TPU v7x, 32 devices: a whole 2x2x4 slice. The times are simulated.
32 devices in a mesh: tower: 2 (over y), narrow: 4 (over z), wide: 4 (over x, core).
Axes of the slice: x: 2, y: 2, z: 4, core: 2. Of those that a mesh axis runs over, the one named last changes fastest.
Arguments:
- features: bfloat16 [4, 8, 256, 2048], P('narrow', ('tower', 'wide')), may hold values from -6 to 6
- w_in: bfloat16 [2048, 4096], P(None, 'narrow'), may hold values from -0.125 to 0.125
- b_in: float32 [4096], P('narrow'), may hold values from -0.5 to 0.5
- w_out: bfloat16 [4096, 256], P('narrow'), may hold values from -0.09375 to 0.09375
- user_emb: bfloat16 [8192, 256], P('narrow'), as said below
- item_ids: int32 [4, 8, 256], P('narrow', ('tower', 'wide')), may hold values from 0 to 8191
Outputs:
- row_loss: float32 [8192], P('narrow')
- item_grad: float32 [4, 8, 256, 256], P('narrow', ('tower', 'wide'))
Inputs may be any that keep to these rules, and one draw needn't show every extreme that they name: `user_emb`: user embeddings.
All inputs are finite; a program needn't handle non-finite values.
Results may differ from a plain program's by a relative error of at most 0.024.
Values may be sent and summed in bfloat16 or wider, within the bound.
A program may use at most 64 MiB of HBM per device.

v0:
```python
import jax
import jax.numpy as jnp
from jax import lax
from jax.sharding import PartitionSpec as P

INV_TEMP = 4.0
EPS = 1e-06
NEG = -1e30


def unit_rows(embed):
    return embed * lax.rsqrt(jnp.sum(embed * embed, axis=1, keepdims=True) + EPS)


def block_scores(user, rid, rglob, vectors, col_ids, col_glob):
    scores = (
        lax.dot_general(user, vectors, (((1,), (1,)), ((), ())), preferred_element_type=jnp.float32)
        * INV_TEMP
    )
    diag = rglob[:, None] == col_glob[None, :]
    keep = (rid[:, None] != col_ids[None, :]) | diag
    return (scores, diag, keep)


def block_scores_cols(vectors, col_ids, col_glob, user, rid, rglob):
    scores = (
        lax.dot_general(vectors, user, (((1,), (1,)), ((), ())), preferred_element_type=jnp.float32)
        * INV_TEMP
    )
    diag = col_glob[:, None] == rglob[None, :]
    keep = (col_ids[:, None] != rid[None, :]) | diag
    return (scores, diag, keep)


def local(features, w_in, b_in, w_out, user_emb, item_ids):
    share = features.shape[2]
    width = features.shape[3]
    embed_width = w_out.shape[1]
    users_dev = user_emb.shape[0]
    groups = lax.axis_size("narrow")
    panel = groups * share
    gathered, gathered_ids = (
        lax.all_gather(features, "narrow", axis=0, tiled=True),
        lax.all_gather(item_ids, "narrow", axis=0, tiled=True),
    )
    rows_in = gathered.reshape(panel, width)
    col_ids = gathered_ids.reshape(panel)
    hidden = jax.nn.relu(jnp.dot(rows_in, w_in, preferred_element_type=jnp.float32) + b_in).astype(
        jnp.bfloat16
    )
    partial_embed = jnp.dot(hidden, w_out, preferred_element_type=jnp.float32)
    item_vec = unit_rows(lax.psum(partial_embed, "narrow")).astype(jnp.bfloat16)
    row_ids = lax.all_gather(item_ids, ("tower", "wide"), axis=1, tiled=True).reshape(users_dev)
    narrow_index = lax.axis_index("narrow")
    panel_index = lax.axis_index(("tower", "wide"))
    row_glob = narrow_index * users_dev + jnp.arange(users_dev, dtype=jnp.int32)
    column = jnp.arange(panel, dtype=jnp.int32)
    col_glob = column // share * users_dev + panel_index * share + column % share
    block = min(512, users_dev)
    count = users_dev // block
    users = user_emb.reshape(count, block, embed_width)
    rid_blocks = row_ids.reshape(count, block)
    rglob_blocks = row_glob.reshape(count, block)

    def local_stats(blk):
        user, rid, rglob = blk
        scores, diag, keep = block_scores(user, rid, rglob, item_vec, col_ids, col_glob)
        masked = jnp.where(keep, scores, NEG)
        top = jnp.max(masked, axis=1)
        mass = jnp.sum(jnp.where(keep, jnp.exp(scores - top[:, None]), 0.0), axis=1)
        pos = jnp.sum(jnp.where(diag, scores, 0.0), axis=1)
        return (top, mass, pos, masked.T)

    def local_stats_only(blk):
        top, mass, pos, masked = local_stats(blk)
        return (top, mass, pos)

    top, mass, pos = lax.map(local_stats_only, (users, rid_blocks, rglob_blocks))
    top = top.reshape(users_dev)
    mass = mass.reshape(users_dev)
    pos = pos.reshape(users_dev)
    global_top = lax.pmax(top, ("tower", "wide"))
    total, global_pos = lax.psum((mass * jnp.exp(top - global_top), pos), ("tower", "wide"))
    lse = global_top + jnp.log(total)
    row_loss = lse - global_pos
    lse_blocks = lse.reshape(count, block)

    def add_block(acc, blk):
        user, rid, rglob, lse_blk = blk
        scores, diag, keep = block_scores_cols(item_vec, col_ids, col_glob, user, rid, rglob)
        coef = (
            jnp.where(keep, jnp.exp(scores - lse_blk[None, :]), 0.0) - diag.astype(jnp.float32)
        ).astype(jnp.bfloat16)
        term = jnp.dot(coef, user, preferred_element_type=jnp.float32)
        return (acc + term, None)

    acc, unused = lax.scan(
        add_block,
        jnp.zeros((share * lax.axis_size("narrow"), embed_width), jnp.float32),
        (users, rid_blocks, rglob_blocks, lse_blocks),
    )
    own_grad = lax.psum_scatter(INV_TEMP * acc, "narrow", scatter_dimension=0, tiled=True)
    return (row_loss, own_grad.reshape(1, 1, share, embed_width))


def solution(mesh):
    return jax.shard_map(
        local,
        mesh=mesh,
        in_specs=(
            P("narrow", ("tower", "wide"), None, None),
            P(None, "narrow"),
            P("narrow"),
            P("narrow", None),
            P("narrow", None),
            P("narrow", ("tower", "wide"), None),
        ),
        out_specs=(P("narrow"), P("narrow", ("tower", "wide"), None, None)),
        check_vma=False,
    )
```

profile of v0, /device:TPU:0, one launch (start us, length us, event | category | flops | bytes accessed | tf_op | source)
XLA Modules:
  0.0 238.5 jit_solution(5663523277225741020)
XLA Ops:
  7.2 0.0 copy-start
  7.2 0.0 all-gather.2.cloned.1.call-start
  7.2 0.7 all-gather.2.cloned.1.call-update
  7.9 0.0 all-reduce.3.cloned.1.call-start
  8.0 85.1 %all-gather.2.cloned.1.call-done = bf16[4,1,256,2048]{3,2,1,0:T(8,128)(2,1)} async-done(((bf16[1,1,256,2048]{3,2,1,0:T(8,128)(2,1)}), bf16[4,1,256,2048]{3,2,1,0:T(8,128)(2,1)}) %all-gather.2.cloned.1.call-update) | async-done | bytes 4194320 | tf_op jit(solution)/shard_map/all_gather | solution.py:43
  93.1 0.0 copy-done
  93.1 0.0 copy-start.1
  93.1 9.6 %fusion.48 = f32[1024,256]{1,0:T(8,128)} fusion(bf16[1024,256]{1,0:T(8,128)(2,1)S(1)} %copy-done, f32[1024]{0:T(1024)} %param.12, bf16[1024,2048]{1,0:T(8,128)(2,1)} %bitcast.95, bf16[2048,1024]{1,0:T(8,128)(2,1)} %param.11), kind=kOutput, calls=%fused_computation.64 | convolution fusion | flops 4834983936 | bytes 9965568 | tf_op jit(solution)/shard_map/dot_general | solution.py:51
  102.7 0.0 copy-start.2
  102.7 0.0 all-reduce.3.cloned.1.call-update
  102.7 0.0 reduce-scatter.2.cloned.1.call-start
  102.8 0.0 copy-done.1
  102.8 9.0 %all_gather.9 = s32[1,8,256]{2,0,1:T(1,128)S(1)} all-gather(s32[1,1,256]{2,0,1:T(1,128)S(1)} %bitcast.94), channel_id=1, replica_groups=mesh['tower'=2,'narrow'=4,'wide'=4] {'tower','wide'}, dimensions={1}, use_global_device_ids=true | all-gather | bytes 9216 | tf_op jit(solution)/shard_map/all_gather | solution.py:53
  111.9 8.8 %all_gather.10 = s32[4,1,256]{2,1,0:T(1,128)S(1)} all-gather(s32[1,1,256]{2,1,0:T(1,128)S(1)} %copy-done.1), channel_id=1, replica_groups=mesh['tower'=2,'narrow'=4,'wide'=4] {'narrow'}, dimensions={0}, use_global_device_ids=true | all-gather | bytes 5120 | tf_op jit(solution)/shard_map/all_gather | solution.py:44
  120.7 32.6 %all-reduce.3.cloned.1.call-done = f32[1024,256]{1,0:T(8,128)} async-done(((f32[1024,256]{1,0:T(8,128)}), f32[1024,256]{1,0:T(8,128)}) %all-reduce.3.cloned.1.call-update) | async-done | bytes 1048592 | tf_op jit(solution)/shard_map/psum | solution.py:52
  153.3 1.4 multiply_reduce_fusion
  154.8 1.4 multiply_convert_fusion
  156.2 0.0 copy-done.2
  156.2 7.8 %while.26 = (s32[]{:T(128)}, f32[4,512]{1,0:T(4,128)S(1)}, f32[4,512]{1,0:T(4,128)S(1)}, f32[4,512]{1,0:T(4,128)S(1)}, s32[4,512]{1,0:T(4,128)S(1)}, /*index=5*/...) while((s32[]{:T(128)}, f32[4,512]{1,0:T(4,128)S(1)}, ...), condition=%wide.region_6.7_spmd.clone, body=%wide.region_2.6_spmd.clone.sunk | while | flops 276313600 | bytes 5038221 | solution.py:78
  156.2 0.7 select_reduce_fusion.3
  156.9 1.1 fusion.70
  158.0 0.1 dynamic_update_slice.17
  158.1 0.1 dynamic_update_slice.16
  158.2 0.7 select_reduce_fusion.3
  158.9 1.1 fusion.70
  160.0 0.1 dynamic_update_slice.17
  160.0 0.1 dynamic_update_slice.16
  160.1 0.7 select_reduce_fusion.3
  160.8 1.1 fusion.70
  162.0 0.1 dynamic_update_slice.17
  162.0 0.1 dynamic_update_slice.16
  162.1 0.7 select_reduce_fusion.3
  162.8 1.1 fusion.70
  163.9 0.1 dynamic_update_slice.17
  164.0 0.1 dynamic_update_slice.16
  164.0 14.1 %pmax.7 = f32[2048]{0:T(1024)S(1)} all-reduce(f32[2048]{0:T(1024)S(1)} %bitcast.84), channel_id=1, replica_groups=mesh['tower'=2,'narrow'=4,'wide'=4] {'tower','wide'}, use_global_device_ids=true, to_apply=%region_7.8 | all-reduce | flops 2048 | bytes 16384 | tf_op jit(solution)/shard_map/pmax | solution.py:82
  178.2 22.3 %all-reduce = (f32[2048]{0:T(1024)S(1)}, f32[2048]{0:T(1024)S(1)}) all-reduce(f32[2048]{0:T(1024)S(1)} %exponential_multiply_fusion, f32[2048]{0:T(1024)S(1)} %bitcast.89), channel_id=1, replica_groups=mesh['tower'=2,'narrow'=4,'wide'=4] {'tower','wide'}, use_global_device_ids=true, to_apply=%region_8.9 | all-reduce | flops 4096 | bytes 32768 | tf_op jit(solution)/shard_map/psum | solution.py:83
  200.5 0.6 fusion.54
  201.1 4.9 %while.27 = (s32[]{:T(128)}, f32[1024,256]{1,0:T(8,128)S(1)}, s32[4,1,256]{2,1,0:T(1,128)S(1)}, s32[4,512]{1,0:T(4,128)S(1)}, s32[4,512]{1,0:T(4,128)S(1)}, /*in...) while((s32[]{:T(128)}, f32[1024,256]{1,0:T(8,128)S(1)}, ...), condition=%wide.region_11.12_spmd.clone, body=%wide.region_10.11_spmd.clone.sunk | while | flops 542129152 | bytes 3177603 | solution.py:97
  201.2 1.2 fusion.75
  202.4 1.2 fusion.75
  203.7 1.2 fusion.75
  204.9 1.2 fusion.75
  206.1 1.1 broadcast_multiply_fusion
  207.1 0.0 reduce-scatter.2.cloned.1.call-update
  207.2 24.8 %reduce-scatter.2.cloned.1.call-done = f32[256,256]{1,0:T(8,128)} async-done(((f32[1024,256]{1,0:T(8,128)}), f32[256,256]{1,0:T(8,128)}) %reduce-scatter.2.cloned.1.call-update) | async-done | bytes 262160 | tf_op jit(solution)/shard_map/reduce_scatter | solution.py:102
  (37 shorter events, 0.5 us)
Async XLA Ops:
  7.2 85.9 %copy-start = (bf16[1024,256]{1,0:T(8,128)(2,1)S(1)}, bf16[1024,256]{1,0:T(8,128)(2,1)}, u32[]{:S(2)}) copy-start(bf16[1024,256]{1,0:T(8,128)(2,1)} %param.13) | copy-start | bytes 1572868
  7.2 85.9 %all-gather.2.cloned.1.call-start = ((), (), s32[]{:S(2)}) async-start(), calls=%async_computation.1 | async-start | bytes 5242880 | tf_op jit(solution)/shard_map/all_gather | solution.py:43
  7.9 145.4 %all-reduce.3.cloned.1.call-start = ((), (), s32[]{:S(2)}) async-start(), calls=%async_computation.2 | async-start | bytes 2097152 | tf_op jit(solution)/shard_map/psum | solution.py:52
  93.1 9.8 %copy-start.1 = (s32[1,1,256]{2,1,0:T(1,128)S(1)}, s32[1,1,256]{2,1,0:T(1,128)}, u32[]{:S(2)}) copy-start(s32[1,1,256]{2,1,0:T(1,128)} %param.15) | copy-start | bytes 3076
  102.7 53.5 %copy-start.2 = (bf16[2048,256]{1,0:T(8,128)(2,1)S(1)}, bf16[2048,256]{1,0:T(8,128)(2,1)}, u32[]{:S(2)}) copy-start(bf16[2048,256]{1,0:T(8,128)(2,1)} %param.14) | copy-start | bytes 3145732
  102.7 129.3 %reduce-scatter.2.cloned.1.call-start = ((), (), s32[]{:S(2)}) async-start(), calls=%async_computation.3 | async-start | bytes 1310720 | tf_op jit(solution)/shard_map/reduce_scatter | solution.py:102
Sparse Core Ops, SparseCore 0:
  9.6 83.4 all-gather.1
  102.9 50.3 all-reduce.2
  207.3 24.6 reduce-scatter.1
where the time goes:
time: 239 us
  waiting for transfers between devices  143 us (60%)
  blocking collectives  54.2 us (23%)
  matrix products  17 us (7%)
  between operations  13.9 us (6%)
  other arithmetic  8.95 us (4%)
    all_gather x1, waiting for transfers between devices, local(): lax.all_gather(features, 'narrow', axis=0, tiled=True)  85.1 us
    psum x1, waiting for transfers between devices, local(): item_vec = unit_rows(lax.psum(partial_embed, 'narrow')).astype(jnp.bfloat16)  32.6 us
    reduce_scatter x1, waiting for transfers between devices, local(): lax.psum_scatter(INV_TEMP * acc, 'narrow', scatter_dimension=0, tiled=True)  24.8 us
    psum x1, blocking collectives, local(): lax.psum((mass * jnp.exp(top - global_top), pos), ('tower', 'wide'))  22.3 us
    pmax x1, blocking collectives, local(): global_top = lax.pmax(top, ('tower', 'wide'))  14.1 us
    dot_general x1, matrix products, local(): partial_embed = jnp.dot(hidden, w_out, preferred_element_type=jnp.float32)  9.62 us
    all_gather x1, blocking collectives, local(): lax.all_gather(item_ids, ('tower', 'wide'), axis=1, tiled=True)  9.02 us
    all_gather x1, blocking collectives, local(): lax.all_gather(item_ids, 'narrow', axis=0, tiled=True)  8.76 us
  transfers between devices with their start and end apart: 3, of which 3 were waited for; matrix products, arithmetic and copies ran while one was open for 0% of the time, Pallas kernels for 0%

commit v1 on v0

--- a/solution.py
+++ b/solution.py
@@ -49,7 +49,9 @@
         jnp.bfloat16
     )
     partial_embed = jnp.dot(hidden, w_out, preferred_element_type=jnp.float32)
-    item_vec = unit_rows(lax.psum(partial_embed, "narrow")).astype(jnp.bfloat16)
+    item_vec = unit_rows(jax.lax.all_gather(partial_embed, axis_name="narrow").sum(axis=0)).astype(
+        jnp.bfloat16
+    )
     row_ids = lax.all_gather(item_ids, ("tower", "wide"), axis=1, tiled=True).reshape(users_dev)
     narrow_index = lax.axis_index("narrow")
     panel_index = lax.axis_index(("tower", "wide"))

time: 239 us -> 275 us (1.15)
  waiting for transfers between devices: 143 us -> 172 us
  matrix products: 17 us -> 24.9 us
    all_gather x0 -> x1, waiting for transfers between devices: none -> 61.9 us  [local(): jax.lax.all_gather(partial_embed, axis_name='narrow').sum(axis=0)]
    psum x1 -> x0, waiting for transfers between devices: 32.6 us -> none  [local(): item_vec = unit_rows(lax.psum(partial_embed, 'narrow')).astype(jnp.bfloat16)]
    dot_general x4, matrix products: 4.65 us -> 8.79 us  [add_block(): term = jnp.dot(coef, user, preferred_element_type=jnp.float32)]
    dot_general x4, matrix products: 2.7 us -> 6.51 us  [block_scores(): lax.dot_general(user, vectors, (((1,), (1,)), ((), ())), preferred_elemen...]
where the time goes in v1:
time: 275 us
  waiting for transfers between devices  172 us (63%)
  blocking collectives  53.7 us (20%)
  matrix products  24.9 us (9%)
  between operations  13.9 us (5%)
  other arithmetic  9.14 us (3%)
    all_gather x1, waiting for transfers between devices, local(): lax.all_gather(features, 'narrow', axis=0, tiled=True)  85.1 us
    all_gather x1, waiting for transfers between devices, local(): jax.lax.all_gather(partial_embed, axis_name='narrow').sum(axis=0)  61.9 us
    reduce_scatter x1, waiting for transfers between devices, local(): lax.psum_scatter(INV_TEMP * acc, 'narrow', scatter_dimension=0, tiled=True)  24.1 us
    psum x1, blocking collectives, local(): lax.psum((mass * jnp.exp(top - global_top), pos), ('tower', 'wide'))  22.3 us
    pmax x1, blocking collectives, local(): global_top = lax.pmax(top, ('tower', 'wide'))  13.9 us
    dot_general x1, matrix products, local(): partial_embed = jnp.dot(hidden, w_out, preferred_element_type=jnp.float32)  9.62 us
    all_gather x1, blocking collectives, local(): lax.all_gather(item_ids, ('tower', 'wide'), axis=1, tiled=True)  8.89 us
    dot_general x4, matrix products, add_block(): term = jnp.dot(coef, user, preferred_element_type=jnp.float32)  8.79 us
  transfers between devices with their start and end apart: 3, of which 3 were waited for; matrix products, arithmetic and copies ran while one was open for 0% of the time, Pallas kernels for 0%

profile of v1, /device:TPU:0, one launch (start us, length us, event | category | flops | bytes accessed | tf_op | source)
XLA Modules:
  0.0 274.6 jit_solution(12173689838555381951)
XLA Ops:
  7.2 0.0 copy-start
  7.2 0.0 all-gather.4.cloned.1.call-start
  7.2 0.7 all-gather.4.cloned.1.call-update
  7.9 0.0 all-gather.6.cloned.1.call-start
  8.0 85.1 %all-gather.4.cloned.1.call-done = bf16[4,1,256,2048]{3,2,1,0:T(8,128)(2,1)} async-done(((bf16[1,1,256,2048]{3,2,1,0:T(8,128)(2,1)}), bf16[4,1,256,2048]{3,2,1,0:T(8,128)(2,1)}) %all-gather.4.cloned.1.call-update) | async-done | bytes 4194320 | tf_op jit(solution)/shard_map/all_gather | solution.py:43
  93.1 0.0 copy-done
  93.1 0.0 copy-start.1
  93.1 9.6 %fusion.48 = f32[1024,256]{1,0:T(8,128)} fusion(bf16[1024,256]{1,0:T(8,128)(2,1)S(1)} %copy-done, f32[1024]{0:T(1024)} %param.12, bf16[1024,2048]{1,0:T(8,128)(2,1)} %bitcast.97, bf16[2048,1024]{1,0:T(8,128)(2,1)} %param.11), kind=kOutput, calls=%fused_computation.64 | convolution fusion | flops 4834983936 | bytes 9965568 | tf_op jit(solution)/shard_map/dot_general | solution.py:51
  102.7 0.0 all-gather.6.cloned.1.call-update
  102.7 0.0 reduce-scatter.2.cloned.1.call-start
  102.8 0.0 copy-done.1
  102.8 8.9 %all_gather.15 = s32[1,8,256]{2,0,1:T(1,128)S(1)} all-gather(s32[1,1,256]{2,0,1:T(1,128)S(1)} %bitcast.96), channel_id=1, replica_groups=mesh['tower'=2,'narrow'=4,'wide'=4] {'tower','wide'}, dimensions={1}, use_global_device_ids=true | all-gather | bytes 9216 | tf_op jit(solution)/shard_map/all_gather | solution.py:55
  111.8 8.5 %all_gather.16 = s32[4,1,256]{2,1,0:T(1,128)S(1)} all-gather(s32[1,1,256]{2,1,0:T(1,128)S(1)} %copy-done.1), channel_id=1, replica_groups=mesh['tower'=2,'narrow'=4,'wide'=4] {'narrow'}, dimensions={0}, use_global_device_ids=true | all-gather | bytes 5120 | tf_op jit(solution)/shard_map/all_gather | solution.py:44
  120.3 61.9 %all-gather.6.cloned.1.call-done = f32[4096,256]{1,0:T(8,128)} async-done(((f32[1024,256]{1,0:T(8,128)}), f32[4096,256]{1,0:T(8,128)}) %all-gather.6.cloned.1.call-update) | async-done | bytes 4194320 | tf_op jit(solution)/shard_map/all_gather | solution.py:52
  182.2 2.6 reduce_sum.36
  184.8 0.2 multiply_reduce_fusion
  185.1 0.2 multiply_convert_fusion
  185.3 11.6 %while.26 = (s32[]{:T(128)}, f32[4,512]{1,0:T(4,128)S(1)}, f32[4,512]{1,0:T(4,128)S(1)}, f32[4,512]{1,0:T(4,128)S(1)}, s32[4,512]{1,0:T(4,128)S(1)}, /*index=5*/...) while((s32[]{:T(128)}, f32[4,512]{1,0:T(4,128)S(1)}, ...), condition=%wide.region_6.7_spmd.clone, body=%wide.region_2.6_spmd.clone.sunk | while | flops 276313600 | bytes 5038729 | solution.py:80
  185.3 1.6 select_reduce_fusion.3
  186.9 1.1 fusion.70
  188.1 0.1 dynamic_update_slice.17
  188.1 0.1 dynamic_update_slice.16
  188.2 1.6 select_reduce_fusion.3
  189.9 1.1 fusion.70
  191.0 0.1 dynamic_update_slice.17
  191.0 0.1 dynamic_update_slice.16
  191.1 1.6 select_reduce_fusion.3
  192.8 1.1 fusion.70
  193.9 0.1 dynamic_update_slice.17
  193.9 0.1 dynamic_update_slice.16
  194.0 1.6 select_reduce_fusion.3
  195.7 1.1 fusion.70
  196.8 0.1 dynamic_update_slice.17
  196.8 0.1 dynamic_update_slice.16
  196.9 13.9 %pmax.7 = f32[2048]{0:T(1024)S(1)} all-reduce(f32[2048]{0:T(1024)S(1)} %bitcast.86), channel_id=1, replica_groups=mesh['tower'=2,'narrow'=4,'wide'=4] {'tower','wide'}, use_global_device_ids=true, to_apply=%region_7.8 | all-reduce | flops 2048 | bytes 16384 | tf_op jit(solution)/shard_map/pmax | solution.py:84
  210.9 22.3 %all-reduce = (f32[2048]{0:T(1024)S(1)}, f32[2048]{0:T(1024)S(1)}) all-reduce(f32[2048]{0:T(1024)S(1)} %exponential_multiply_fusion, f32[2048]{0:T(1024)S(1)} %bitcast.91), channel_id=1, replica_groups=mesh['tower'=2,'narrow'=4,'wide'=4] {'tower','wide'}, use_global_device_ids=true, to_apply=%region_8.9 | all-reduce | flops 4096 | bytes 32768 | tf_op jit(solution)/shard_map/psum | solution.py:85
  233.2 0.6 fusion.54
  233.8 9.1 %while.27 = (s32[]{:T(128)}, f32[1024,256]{1,0:T(8,128)S(1)}, s32[4,1,256]{2,1,0:T(1,128)S(1)}, s32[4,512]{1,0:T(4,128)S(1)}, s32[4,512]{1,0:T(4,128)S(1)}, /*in...) while((s32[]{:T(128)}, f32[1024,256]{1,0:T(8,128)S(1)}, ...), condition=%wide.region_11.12_spmd.clone, body=%wide.region_10.11_spmd.clone.sunk | while | flops 542129152 | bytes 3177603 | solution.py:99
  233.9 2.2 fusion.75
  236.2 2.2 fusion.75
  238.5 2.2 fusion.75
  240.7 2.2 fusion.75
  242.9 1.1 broadcast_multiply_fusion
  244.0 0.0 reduce-scatter.2.cloned.1.call-update
  244.0 24.1 %reduce-scatter.2.cloned.1.call-done = f32[256,256]{1,0:T(8,128)} async-done(((f32[1024,256]{1,0:T(8,128)}), f32[256,256]{1,0:T(8,128)}) %reduce-scatter.2.cloned.1.call-update) | async-done | bytes 262160 | tf_op jit(solution)/shard_map/reduce_scatter | solution.py:104
  (37 shorter events, 0.5 us)
Async XLA Ops:
  7.2 85.9 %copy-start = (bf16[1024,256]{1,0:T(8,128)(2,1)S(1)}, bf16[1024,256]{1,0:T(8,128)(2,1)}, u32[]{:S(2)}) copy-start(bf16[1024,256]{1,0:T(8,128)(2,1)} %param.13) | copy-start | bytes 1572868
  7.2 85.9 %all-gather.4.cloned.1.call-start = ((), (), s32[]{:S(2)}) async-start(), calls=%async_computation.1 | async-start | bytes 5242880 | tf_op jit(solution)/shard_map/all_gather | solution.py:43
  7.9 174.3 %all-gather.6.cloned.1.call-start = ((), (), s32[]{:S(2)}) async-start(), calls=%async_computation.3 | async-start | bytes 5242880 | tf_op jit(solution)/shard_map/all_gather | solution.py:52
  93.1 9.7 %copy-start.1 = (s32[1,1,256]{2,1,0:T(1,128)S(1)}, s32[1,1,256]{2,1,0:T(1,128)}, u32[]{:S(2)}) copy-start(s32[1,1,256]{2,1,0:T(1,128)} %param.15) | copy-start | bytes 3076
  102.7 165.3 %reduce-scatter.2.cloned.1.call-start = ((), (), s32[]{:S(2)}) async-start(), calls=%async_computation.2 | async-start | bytes 1310720 | tf_op jit(solution)/shard_map/reduce_scatter | solution.py:104
Sparse Core Ops, SparseCore 0:
  9.6 83.4 all-gather.3
  102.9 79.3 all-gather.5
  244.1 23.9 reduce-scatter.1
